TPU v7x, 32 devices: a whole 2x2x4 slice. The times are simulated.
32 devices in a mesh: beam: 2 (over y), chan: 4 (over z), tile: 2 (over x), pol: 2 (over core).
Axes of the slice: x: 2, y: 2, z: 4, core: 2. Of those that a mesh axis runs over, the one named last changes fastest.
Arguments:
- voltages: bfloat16 [8, 32, 100000], P(('beam', 'tile', 'pol'), 'chan'), parts along dimension 0, may hold values from -6 to 6
- flagged: int32 [4, 32], P(('tile', 'pol'), 'chan'), may hold values 0 or 1
- channel_table: int32 [4], replicated, may hold values from 0 to 3, each once
Outputs:
- visibilities: float32 [2, 8, 128, 128], P(None, ('beam', 'chan'), ('tile', 'pol')), parts along dimension 1
There are 2 independent parts, one for each index of `beam`. A program takes and returns all parts, laid end to end along the dimension named above; an argument that names none is the same for every part. Nothing has to cross between parts.
Inputs may be any that keep to these rules, and one draw needn't show every extreme that they name: `flagged`: 1 marks an input whose spectra are zeroed. `channel_table`: a permutation of the 4 channel blocks.
All inputs are finite; a program needn't handle non-finite values. No bound on the sum of `flagged` on one device may be relied on, other than what follows from the above.
Results may differ from a plain program's by a relative error of at most 0.0012.
Values may be sent and summed in bfloat16 or wider, within the bound.
A program may use at most 64 MiB of HBM per device.

v0:
```python
import math

import jax
import jax.numpy as jnp
import numpy as np
from jax import lax
from jax.sharding import PartitionSpec as P

N_OUTER = 160
N_INNER = 125
TAPS = 4
FRAMES = 2


def window_table(tap_count, frame_len):
    position = np.arange(tap_count * frame_len) * 1.0
    centre = (position - tap_count * frame_len / 2.0 + 0.5) / frame_len
    shaped = np.sin(np.pi * centre) / (np.pi * centre)
    prototype = shaped * (
        0.5 - 0.5 * np.cos(2.0 * np.pi * (position + 0.5) / (tap_count * frame_len))
    )
    prototype = prototype / np.sqrt(np.sum(prototype * prototype) / frame_len)
    return prototype.reshape(tap_count, frame_len)


def make_spectra(samples_in, flags_in, channel_table, n_chan):
    in_dev = samples_in.shape[0]
    frame_len = N_OUTER * N_INNER
    half_len = N_OUTER // 2
    filt = jnp.asarray(window_table(TAPS, frame_len), jnp.float32)
    frames_all = samples_in.astype(jnp.float32).reshape(in_dev, FRAMES + TAPS - 1, frame_len)
    filtered = jnp.zeros((in_dev, FRAMES, frame_len), jnp.float32)
    for tap_index in range(TAPS):
        filtered = filtered + filt[tap_index] * frames_all[:, tap_index : tap_index + FRAMES]
    filtered = filtered.reshape(in_dev, FRAMES, N_INNER, N_OUTER)
    inner_idx = jnp.arange(N_INNER, dtype=jnp.int32)
    inner_ang = (
        2.0
        * math.pi
        / N_INNER
        * (inner_idx[:, None] * inner_idx[None, :] % N_INNER).astype(jnp.float32)
    )
    inner_mat = jnp.concatenate([jnp.cos(inner_ang), -jnp.sin(inner_ang)], axis=0)
    section_one = jnp.einsum("kn,vsnm->vskm", inner_mat, filtered, precision=lax.Precision.HIGH)
    real_one = section_one[:, :, :N_INNER]
    imag_one = section_one[:, :, N_INNER:]
    outer_idx = jnp.arange(N_OUTER, dtype=jnp.int32)
    twist_ang = (
        2.0
        * math.pi
        / frame_len
        * (inner_idx[:, None] * outer_idx[None, :] % frame_len).astype(jnp.float32)
    )
    twist_cos = jnp.cos(twist_ang)
    twist_sin = jnp.sin(twist_ang)
    real_two = real_one * twist_cos + imag_one * twist_sin
    imag_two = imag_one * twist_cos - real_one * twist_sin
    joined = jnp.concatenate([real_two, imag_two], axis=3)
    block_width = half_len // n_chan
    out_pos = jnp.arange(half_len, dtype=jnp.int32)
    owner = out_pos // block_width
    onehot = owner[:, None] == jnp.arange(n_chan, dtype=jnp.int32)[None, :]
    chosen = jnp.sum(jnp.where(onehot, channel_table[None, :], 0), axis=1)
    outer_k = chosen * block_width + out_pos % block_width
    outer_ang = (
        2.0
        * math.pi
        / N_OUTER
        * (outer_k[:, None] * outer_idx[None, :] % N_OUTER).astype(jnp.float32)
    )
    outer_cos = jnp.cos(outer_ang)
    outer_sin = jnp.sin(outer_ang)
    real_rows = jnp.concatenate([outer_cos, outer_sin], axis=1)
    imag_rows = jnp.concatenate([-outer_sin, outer_cos], axis=1)
    outer_mat = jnp.stack([real_rows, imag_rows], axis=0)
    spectrum = jnp.einsum("vskn,rjn->vrsjk", joined, outer_mat, precision=lax.Precision.HIGH)
    spectrum = spectrum.reshape(in_dev, 2, FRAMES, half_len * N_INNER)
    kept_mask = (1 - flags_in).astype(jnp.float32)
    spectrum = spectrum * (kept_mask[:, None, None, None] / math.sqrt(frame_len))
    return spectrum.astype(jnp.bfloat16)


def correlate(left_rows, panel_cols, scale):
    return (
        jnp.einsum("rik,jk->rij", left_rows, panel_cols, preferred_element_type=jnp.float32) * scale
    )


def on_device(voltages, flagged, channel_table):
    n_chan = lax.axis_size("chan")
    spectra = make_spectra(voltages[0], flagged[0], channel_table, n_chan)
    turned = lax.all_to_all(spectra, "chan", split_axis=3, concat_axis=0, tiled=True)
    group_len = turned.shape[0]
    chb_len = turned.shape[3]
    half_k = FRAMES * chb_len
    scale = 1.0 / math.sqrt(FRAMES * chb_len)
    band_rows = turned.reshape(group_len, 2 * half_k)
    swapped = jnp.concatenate([band_rows[:, half_k:], -band_rows[:, :half_k]], axis=1)
    left_rows = jnp.stack([band_rows, swapped], axis=0)
    vis_local = correlate(
        left_rows, lax.all_gather(band_rows, ("tile", "pol"), axis=0, tiled=True), scale
    )
    return vis_local[:, None]


def solution(mesh):
    in_specs = (P(("beam", "tile", "pol"), "chan", None), P(("tile", "pol"), "chan"), P())
    out_specs = P(None, ("beam", "chan"), ("tile", "pol"), None)
    return jax.shard_map(
        on_device, mesh=mesh, in_specs=in_specs, out_specs=out_specs, check_vma=False
    )
```

profile of v0, /device:TPU:0, one launch (start us, length us, event | category | flops | bytes accessed | tf_op | source)
XLA Modules:
  0.0 155.5 jit_solution(12879074996876843924)
XLA Ops:
  6.5 0.9 sine_negate_fusion
  7.5 1.0 fusion.38
  8.5 0.7 multiply_bitcast_fusion
  9.2 0.7 select_reduce_fusion
  9.9 1.1 fusion.42
  11.0 5.3 %reshape.90 = f32[8,5,20000]{2,1,0:T(8,128)} reshape(bf16[1,8,100000]{2,1,0:T(8,128)(2,1)} %param.4) | data formatting | bytes 4800000 | tf_op jit(solution)/shard_map/convert_element_type | solution.py:31
  16.3 10.0 %fusion.57 = (f32[8,2,20000]{2,1,0:T(2,128)S(1)}, f32[8,2,20000]{2,1,0:T(2,128)S(1)}, f32[8,2,20000]{2,1,0:T(2,128)S(1)}, f32[8,2,20000]{2,1,0:T(2,128)S(1)}) fusion(f32[8,5,20000]{2,1,0:T(8,128)} %reshape.90), kind=kLoop, calls=%fused_computation.76 | loop fusion | bytes 10240000 | tf_op jit(solution)/shard_map/slice | solution.py:34
  26.4 0.5 fusion.15
  26.9 1.3 reshape.87
  28.2 1.1 maximum_bitcast_fusion.9
  29.3 2.8 %fusion.7 = f32[8,2,250,160]{2,3,1,0:T(8,128)S(1)} fusion(f32[8,2,125,160]{3,2,0,1:T(8,128)S(1)} %reshape.87, f32[125,125]{1,0:T(8,128)} %get-tuple-element.18, f32[125,125]{1,0:T(8,128)} %get-tuple-element.19), kind=kOutput, calls=%fused_computation.8 | convolution fusion | flops 480031232 | bytes 3965000 | tf_op jit(solution)/shard_map/kn,vsnm->vskm/dot_general | solution.py:44
  32.1 0.7 multiply_add_fusion
  32.8 1.2 fusion.10
  34.1 1.7 %reshape.95 = f32[8,2,2,10000]{3,2,0,1:T(2,128)S(1)} reshape(f32[8,2,2,80,125]{4,3,2,0,1:T(8,128)S(1)} %fusion.10) | data formatting | bytes 2560000 | tf_op jit(solution)/shard_map/reshape | solution.py:77
  35.9 16.1 %copy.32 = bf16[8,2,2,10000]{0,2,1,3:T(2,128)(2,1)} copy(bf16[8,2,2,10000]{3,0,2,1:T(8,128)(2,1)S(1)} %fusion.14) | data formatting | bytes 1280000 | tf_op jit(solution)/shard_map/convert_element_type | solution.py:80
  52.0 13.1 %reshape.96 = bf16[4,2,40000]{2,1,0:T(2,128)(2,1)S(1)} reshape(bf16[10000,2,2,8]{3,2,1,0:T(2,128)(2,1)} %bitcast.48) | data formatting | bytes 1280000
  65.2 23.1 %all_to_all.15 = bf16[4,2,40000]{2,1,0:T(2,128)(2,1)S(1)} all-to-all(bf16[4,2,40000]{2,1,0:T(2,128)(2,1)S(1)} %reshape.96), channel_id=1, replica_groups=mesh['beam'=2,'chan'=4,'tile'=2,'pol'=2] {'chan'}, dimensions={0} | all-to-all | bytes 1280000 | tf_op jit(solution)/shard_map/all_to_all | solution.py:92
  88.3 11.1 %reshape.97 = bf16[10000,2,2,8]{3,2,1,0:T(2,128)(2,1)} reshape(bf16[4,2,40000]{2,1,0:T(2,128)(2,1)S(1)} %all_to_all.15) | data formatting | bytes 1280000
  99.3 19.7 %copy.33 = bf16[8,2,2,4,2500]{4,2,1,0,3:T(2,128)(2,1)S(1)} copy(bf16[8,2,2,4,2500]{0,2,1,4,3:T(2,128)(2,1)} %bitcast.49) | data formatting | bytes 1280000 | tf_op jit(solution)/shard_map/all_to_all | solution.py:92
  119.1 1.5 reshape.89
  120.6 0.7 stack_reshape.3
  121.4 0.3 copy-done
  122.0 23.3 %all-gather.2.cloned.1.call-done = bf16[128,10000]{1,0:T(8,128)(2,1)} async-done(((bf16[32,10000]{1,0:T(8,128)(2,1)}), bf16[128,10000]{1,0:T(8,128)(2,1)}) %all-gather.2.cloned.1.call-update) | async-done | bytes 2560016 | tf_op jit(solution)/shard_map/all_gather | solution.py:101
  145.3 3.4 %fusion.23 = f32[2,1,32,128]{3,2,1,0:T(8,128)} fusion(bf16[128,10000]{1,0:T(8,128)(2,1)} %all-gather.2.cloned.1.call-done, bf16[1,32,10000]{2,1,0:T(8,128)(2,1)S(1)} %maximum_bitcast_fusion.4, bf16[1,32,10000]{2,1,0:T(8,128)(2,1)S(1)} %stack_reshape.3), kind=kOutput, calls=%fused_computation.25 | convolution fusion | flops 164488192 | bytes 3872768 | tf_op jit(solution)/shard_map/rik,jk->rij/dot_general | solution.py:85
  (20 shorter events, 0.5 us)
Async XLA Ops:
  6.5 138.7 %all-gather.2.cloned.1.call-start = ((), (), s32[]{:S(2)}) async-start(), calls=%async_computation.1 | async-start | bytes 3235840 | tf_op jit(solution)/shard_map/all_gather | solution.py:101
  16.3 10.1 %copy-start.3 = (f32[20000]{0:T(1024)S(1)}, f32[20000]{0:T(1024)}, u32[]{:S(2)}) copy-start(f32[20000]{0:T(1024)} %constant.79) | copy-start | bytes 240004
  16.3 10.1 %copy-start.4 = (f32[20000]{0:T(1024)S(1)}, f32[20000]{0:T(1024)}, u32[]{:S(2)}) copy-start(f32[20000]{0:T(1024)} %constant.77) | copy-start | bytes 240004
  16.3 10.1 %copy-start.5 = (f32[20000]{0:T(1024)S(1)}, f32[20000]{0:T(1024)}, u32[]{:S(2)}) copy-start(f32[20000]{0:T(1024)} %constant.75) | copy-start | bytes 240004
  16.3 10.1 %copy-start.6 = (f32[20000]{0:T(1024)S(1)}, f32[20000]{0:T(1024)}, u32[]{:S(2)}) copy-start(f32[20000]{0:T(1024)} %constant.73) | copy-start | bytes 240004
  29.3 2.8 %copy-start.1 = (f32[125,160]{0,1:T(8,128)S(1)}, f32[125,160]{0,1:T(8,128)}, u32[]{:S(2)}) copy-start(f32[125,160]{0,1:T(8,128)} %get-tuple-element.20) | copy-start | bytes 240004
  29.3 2.8 %copy-start.2 = (f32[125,160]{0,1:T(8,128)S(1)}, f32[125,160]{0,1:T(8,128)}, u32[]{:S(2)}) copy-start(f32[125,160]{0,1:T(8,128)} %get-tuple-element.21) | copy-start | bytes 240004
  120.6 1.1 copy-start
Sparse Core Ops, SparseCore 0:
  120.8 24.4 all-gather.1
where the time goes:
time: 156 us; the launch traced here: 155 us
  local copies, waits for them, and re-layouts  81 us (52%)
  waiting for transfers between devices  23.3 us (15%)
  blocking collectives  23.1 us (15%)
  between operations  13.5 us (9%)
  matrix products  7.41 us (5%)
  other arithmetic  7.17 us (5%)
    unnamed x16, local copies, waits for them, and re-layouts  24.6 us
    all_gather x1, waiting for transfers between devices, on_device(): lax.all_gather(band_rows, ('tile', 'pol'), axis=0, tiled=True)  23.3 us
    all_to_all x1, blocking collectives, on_device(): lax.all_to_all(spectra, 'chan', split_axis=3, concat_axis=0, tiled=True)  23.1 us
    all_to_all x1, local copies, waits for them, and re-layouts, on_device(): lax.all_to_all(spectra, 'chan', split_axis=3, concat_axis=0, tiled=True)  19.7 us
    convert_element_type x1, local copies, waits for them, and re-layouts, make_spectra(): return spectrum.astype(jnp.bfloat16)  16.1 us
    slice x1, local copies, waits for them, and re-layouts, make_spectra(): frames_all[:, tap_index:tap_index + FRAMES]  10 us
    convert_element_type x1, local copies, waits for them, and re-layouts, make_spectra(): samples_in.astype(jnp.float32).reshape(in_dev, FRAMES + TAPS - 1, frame_len)  5.31 us
    dot_general x1, matrix products, correlate(): jnp.einsum('rik,jk->rij', left_rows, panel_cols, preferred_element_type=j...  3.36 us
  transfers between devices with their start and end apart: 1, of which 1 were waited for; matrix products, arithmetic and copies ran while one was open for 1% of the time, Pallas kernels for 0%

commit v1 on v0

--- a/solution.py
+++ b/solution.py
@@ -1,9 +1,12 @@
+import functools
 import math
 
 import jax
 import jax.numpy as jnp
 import numpy as np
 from jax import lax
+from jax.experimental import pallas as pl
+from jax.experimental.pallas import tpu as pltpu
 from jax.sharding import PartitionSpec as P
 
 N_OUTER = 160
@@ -103,9 +106,287 @@
     return vis_local[:, None]
 
 
+MESH = pl.DeviceIdType.MESH
+LANES = 128
+A_LEN = 625
+A_PAD = 640
+K0_HALF = 313
+K0_PAD = 320
+R_ALL = 16
+IN_DEV = 8
+HALF_IN = 4
+ROWS = 16
+WIDE = FRAMES * K0_PAD
+
+
+def split_bf16(table):
+    high = table.astype(jnp.bfloat16)
+    low = (table - high.astype(np.float64)).astype(jnp.bfloat16)
+    return high, low
+
+
+def tables(n_groups, n_chan):
+    frame_len = N_OUTER * N_INNER
+    window = window_table(TAPS, frame_len).reshape(-1).astype(np.float32).astype(np.float64)
+    shift = frame_len // LANES
+    win = np.zeros((FRAMES, A_PAD * LANES))
+    win[0, : window.size] = window
+    offset = frame_len - shift * LANES
+    win[1, offset : offset + window.size] = window
+    win = win.reshape(FRAMES, A_PAD, LANES)
+
+    k0 = np.arange(K0_HALF)
+    a = np.arange(A_LEN + 1)
+    ang = 2.0 * np.pi / A_LEN * ((4 * k0[:, None] * a[None, :]) % A_LEN)
+    dft = np.zeros((2, K0_PAD, A_PAD))
+    dft[0, :K0_HALF, : A_LEN + 1] = np.cos(ang)
+    dft[1, :K0_HALF, : A_LEN + 1] = -np.sin(ang)
+    dft = dft.reshape(2 * K0_PAD, A_PAD)
+
+    b = np.arange(LANES)
+    twist = np.zeros((FRAMES, 2, K0_PAD, LANES))
+    for s in range(FRAMES):
+        first = s * shift * LANES
+        ang = 2.0 * np.pi / frame_len * ((k0[:, None] * (b[None, :] + first)) % frame_len)
+        twist[s, 0, :K0_HALF] = np.cos(ang)
+        twist[s, 1, :K0_HALF] = np.sin(ang)
+    twist = twist / math.sqrt(frame_len)
+
+    r = np.arange(R_ALL)
+    ang = 2.0 * np.pi / 32 * ((r[:, None] * b[None, :]) % 32)
+    mir = 2.0 * np.pi / 32 * (((31 - r)[:, None] * b[None, :]) % 32)
+    outer = np.zeros((R_ALL, 4, 2, LANES))
+    outer[:, 0, 0], outer[:, 0, 1] = np.cos(ang), np.sin(ang)
+    outer[:, 1, 0], outer[:, 1, 1] = -np.sin(ang), np.cos(ang)
+    outer[:, 2, 0], outer[:, 2, 1] = np.cos(mir), np.sin(mir)
+    outer[:, 3, 0], outer[:, 3, 1] = np.sin(mir), -np.cos(mir)
+    outer = outer.reshape(n_chan, n_groups * 4, 2 * LANES)
+    outer = np.stack(split_bf16(outer), axis=1)
+
+    n_src = n_groups * n_chan
+    perm = np.zeros((4, n_src * IN_DEV, 2, n_src, 4, HALF_IN))
+    for src in range(n_src):
+        for h in range(2):
+            for i in range(HALF_IN):
+                for q in range(4):
+                    perm[q, src * IN_DEV + h * HALF_IN + i, h, src, q, i] = 1.0
+    size = 4 * n_src * IN_DEV
+    perm = perm.reshape(size, size).astype(jnp.bfloat16)
+    dft_high, dft_low = split_bf16(dft)
+    return win.astype(np.float32), dft_high, dft_low, twist.astype(np.float32), outer, perm
+
+
+def kernel(
+    n_chan, n_tile, n_pol, volt_ref, flag_ref, table_ref, win_ref, dh_ref, dl_ref, twist_ref,
+    outer_ref, perm_ref, out_ref, flat, u_high, u_low, zt, turned, send, recv, left, vpart, vrecv,
+    send_sem, recv_sem, vsend_sem, vrecv_sem,
+):
+    n_groups = n_tile * n_pol
+    c, t, p = lax.axis_index("chan"), lax.axis_index("tile"), lax.axis_index("pol")
+    g = t * n_pol + p
+    src = g * n_chan + c
+
+    def peers():
+        found = []
+        for dc in range(n_chan - 1, -1, -1):
+            for dt in range(n_tile - 1, -1, -1):
+                for dp in range(n_pol - 1, -1, -1):
+                    if dc or dt or dp:
+                        found.append(((c + dc) % n_chan, (t + dt) % n_tile, (p + dp) % n_pol))
+        return found
+
+    def where(peer):
+        return {"chan": peer[0], "tile": peer[1], "pol": peer[2]}
+
+    everyone = peers()
+    barrier = pltpu.get_barrier_semaphore()
+    for peer in everyone:
+        pl.semaphore_signal(barrier, inc=1, device_id=where(peer), device_id_type=MESH)
+
+    tiles_full = volt_ref.shape[2] // LANES
+    rest = volt_ref.shape[2] - tiles_full * LANES
+    flat[pl.ds(tiles_full * IN_DEV, flat.shape[0] - tiles_full * IN_DEV), :] = jnp.zeros(
+        (flat.shape[0] - tiles_full * IN_DEV, LANES), jnp.float32
+    )
+    if rest:
+        flat[pl.ds(tiles_full * IN_DEV, IN_DEV), pl.ds(0, rest)] = volt_ref[
+            0, :, pl.ds(tiles_full * LANES, rest)
+        ].astype(jnp.float32)
+
+    step = 11
+
+    def spread(chunk, carry):
+        for j in range(step):
+            tile = chunk * step + j
+            lane = pl.multiple_of(tile * LANES, LANES)
+            row = pl.multiple_of(tile * IN_DEV, IN_DEV)
+            flat[pl.ds(row, IN_DEV), :] = volt_ref[0, :, pl.ds(lane, LANES)].astype(jnp.float32)
+        return carry
+
+    lax.fori_loop(0, tiles_full // step, spread, 0)
+
+    outer_rows = jnp.concatenate(
+        [outer_ref[table_ref[b], part] for part in range(2) for b in range(n_chan)], axis=0
+    )
+    shift = N_OUTER * N_INNER // LANES
+    n_rows = R_ALL * 4
+    row_id = lax.broadcasted_iota(jnp.int32, (n_rows, WIDE), 0)
+    lane_id = lax.broadcasted_iota(jnp.int32, (n_rows, WIDE), 1)
+    twice = ((row_id % 4) >= 2) & ((lane_id == 0) | (lane_id == K0_PAD))
+    once = jnp.where(twice, 0.0, 1.0)
+
+    for h in range(2):
+        for i in range(HALF_IN):
+            for s in range(FRAMES):
+                first = s * shift * IN_DEV + h * HALF_IN + i
+                col = (i * FRAMES + s) * LANES
+                u = flat[pl.ds(first, A_PAD, stride=IN_DEV), :] * win_ref[s]
+                high = u.astype(jnp.bfloat16)
+                u_high[:, col : col + LANES] = high
+                u_low[:, col : col + LANES] = (u - high.astype(jnp.float32)).astype(jnp.bfloat16)
+        for i in range(HALF_IN):
+            for s in range(FRAMES):
+                col = (i * FRAMES + s) * LANES
+                if s == 0:
+                    wide = pl.ds(i * FRAMES * LANES, FRAMES * LANES)
+                    uh, ul = u_high[:, wide], u_low[:, wide]
+                    y = (
+                        jnp.dot(dh_ref[...], uh, preferred_element_type=jnp.float32)
+                        + jnp.dot(dl_ref[...], uh, preferred_element_type=jnp.float32)
+                        + jnp.dot(dh_ref[...], ul, preferred_element_type=jnp.float32)
+                    )
+                yr = y[:K0_PAD, s * LANES : (s + 1) * LANES]
+                yi = y[K0_PAD:, s * LANES : (s + 1) * LANES]
+                co, si = twist_ref[s, 0], twist_ref[s, 1]
+                zt[i % 2, pl.ds(s * K0_PAD, K0_PAD), 0:LANES] = (yr * co + yi * si).astype(jnp.bfloat16)
+                zt[i % 2, pl.ds(s * K0_PAD, K0_PAD), LANES : 2 * LANES] = (yi * co - yr * si).astype(
+                    jnp.bfloat16
+                )
+            x = lax.dot_general(
+                outer_rows, zt[i % 2], (((1,), (1,)), ((), ())), preferred_element_type=jnp.float32
+            )
+            keep = (1 - flag_ref[0, h * HALF_IN + i]).astype(jnp.float32)
+            x = (x[:n_rows] + x[n_rows:]) * (once * keep)
+            for l in range(WIDE // LANES):
+                turned[l, pl.ds(i, n_rows, stride=HALF_IN), :] = x[:, l * LANES : (l + 1) * LANES]
+        for l in range(WIDE // LANES):
+            send[h, :, :, pl.ds(l * LANES, LANES)] = (
+                turned[l].astype(jnp.bfloat16).reshape(R_ALL, ROWS, LANES)
+            )
+        if h == 0:
+            pl.semaphore_wait(barrier, len(everyone))
+        for d, peer in enumerate(everyone):
+            slot = peer[0] * n_groups + peer[1] * n_pol + peer[2]
+            pltpu.make_async_remote_copy(
+                src_ref=send.at[h, slot],
+                dst_ref=recv.at[h, src],
+                send_sem=send_sem.at[h, d],
+                recv_sem=recv_sem.at[h, d],
+                device_id=where(peer),
+                device_id_type=MESH,
+            ).start()
+        recv[h, src] = send[h, c * n_groups + g]
+
+    for h in range(2):
+        for d, peer in enumerate(everyone):
+            slot = peer[0] * n_groups + peer[1] * n_pol + peer[2]
+            pltpu.make_async_remote_copy(
+                src_ref=send.at[h, slot],
+                dst_ref=recv.at[h, src],
+                send_sem=send_sem.at[h, d],
+                recv_sem=recv_sem.at[h, d],
+                device_id=where(peer),
+                device_id_type=MESH,
+            ).wait()
+
+    n_in = n_groups * n_chan * IN_DEV
+    got = recv[...].reshape(4 * n_in, WIDE)
+    for q in range(4):
+        part = jnp.dot(
+            perm_ref[pl.ds(q * n_in, n_in), :], got, preferred_element_type=jnp.float32
+        ).astype(jnp.bfloat16)
+        left[0:n_in, pl.ds(q * WIDE, WIDE)] = part
+        if q % 2 == 0:
+            left[n_in : 2 * n_in, pl.ds((q + 1) * WIDE, WIDE)] = -part
+        else:
+            left[n_in : 2 * n_in, pl.ds((q - 1) * WIDE, WIDE)] = part
+    vis = lax.dot_general(
+        left[...], left[0:n_in, :], (((1,), (1,)), ((), ())), preferred_element_type=jnp.float32
+    )
+    vis = vis * (1.0 / math.sqrt(FRAMES * n_groups * A_LEN))
+    rows = n_in // n_groups
+    for k in range(n_groups):
+        vpart[k, 0:rows] = vis[k * rows : (k + 1) * rows]
+        vpart[k, rows : 2 * rows] = vis[n_in + k * rows : n_in + (k + 1) * rows]
+
+    moves = []
+    for dt in range(n_tile - 1, -1, -1):
+        for dp in range(n_pol - 1, -1, -1):
+            if dt or dp:
+                pt, pp = (t + dt) % n_tile, (p + dp) % n_pol
+                d = len(moves)
+                move = pltpu.make_async_remote_copy(
+                    src_ref=vpart.at[pt * n_pol + pp],
+                    dst_ref=vrecv.at[d],
+                    send_sem=vsend_sem.at[d],
+                    recv_sem=vrecv_sem.at[d],
+                    device_id={"tile": pt, "pol": pp},
+                    device_id_type=MESH,
+                )
+                move.start()
+                moves.append(move)
+    total = vpart[g]
+    for d, move in enumerate(moves):
+        move.wait()
+        total = total + vrecv[d]
+    out_ref[0, 0] = total[:rows]
+    out_ref[1, 0] = total[rows:]
+
+
+def on_device_kernel(n_chan, n_tile, n_pol, voltages, flagged, channel_table):
+    n_groups = n_tile * n_pol
+    n_src = n_groups * n_chan
+    n_in = n_src * IN_DEV
+    consts = [jnp.asarray(x) for x in tables(n_groups, n_chan)]
+    vmem = pl.BlockSpec(memory_space=pltpu.VMEM)
+    smem = pl.BlockSpec(memory_space=pltpu.SMEM)
+    rows = n_in // n_groups
+    tiles = -(-voltages.shape[2] // LANES)
+    tall = max(tiles, N_OUTER * N_INNER // LANES + A_PAD)
+    return pl.pallas_call(
+        functools.partial(kernel, n_chan, n_tile, n_pol),
+        out_shape=jax.ShapeDtypeStruct((2, 1, rows, n_in), jnp.float32),
+        in_specs=[vmem, smem, smem] + [vmem] * 6,
+        out_specs=vmem,
+        scratch_shapes=[
+            pltpu.VMEM((tall * IN_DEV, LANES), jnp.float32),
+            pltpu.VMEM((A_PAD, HALF_IN * FRAMES * LANES), jnp.bfloat16),
+            pltpu.VMEM((A_PAD, HALF_IN * FRAMES * LANES), jnp.bfloat16),
+            pltpu.VMEM((2, WIDE, 2 * LANES), jnp.bfloat16),
+            pltpu.VMEM((WIDE // LANES, R_ALL * ROWS, LANES), jnp.float32),
+            pltpu.VMEM((2, R_ALL, ROWS, WIDE), jnp.bfloat16),
+            pltpu.VMEM((2, n_src, ROWS, WIDE), jnp.bfloat16),
+            pltpu.VMEM((2 * n_in, 4 * WIDE), jnp.bfloat16),
+            pltpu.VMEM((n_groups, 2 * rows, n_in), jnp.float32),
+            pltpu.VMEM((n_groups - 1, 2 * rows, n_in), jnp.float32),
+            pltpu.SemaphoreType.DMA((2, n_src - 1)),
+            pltpu.SemaphoreType.DMA((2, n_src - 1)),
+            pltpu.SemaphoreType.DMA((n_groups - 1,)),
+            pltpu.SemaphoreType.DMA((n_groups - 1,)),
+        ],
+        compiler_params=pltpu.CompilerParams(
+            collective_id=0, has_side_effects=True, vmem_limit_bytes=48 * 1024 * 1024
+        ),
+    )(voltages, flagged, channel_table, *consts)
+
+
 def solution(mesh):
+    n_chan, n_tile, n_pol = mesh.shape["chan"], mesh.shape["tile"], mesh.shape["pol"]
+    body = on_device
+    if n_chan * n_tile * n_pol == R_ALL:
+        body = functools.partial(on_device_kernel, n_chan, n_tile, n_pol)
     in_specs = (P(("beam", "tile", "pol"), "chan", None), P(("tile", "pol"), "chan"), P())
     out_specs = P(None, ("beam", "chan"), ("tile", "pol"), None)
     return jax.shard_map(
-        on_device, mesh=mesh, in_specs=in_specs, out_specs=out_specs, check_vma=False
-    )
+        body, mesh=mesh, in_specs=in_specs, out_specs=out_specs, check_vma=False
+    )

time: 156 us -> 45.1 us (0.29)
  local copies, waits for them, and re-layouts: 81 us -> 9.69 us
  Pallas kernels: 0 us -> 35 us
  waiting for transfers between devices: 23.3 us -> 0 us
  blocking collectives: 23.1 us -> 0 us
  between operations: 13.5 us -> 0.02 us
  matrix products: 7.41 us -> 0 us
  other arithmetic: 7.17 us -> 0 us
    pallas_call x0 -> x1, Pallas kernels: none -> 35 us  [on_device_kernel(): pl.pallas_call(functools.partial(kernel, n_chan, n_tile, n_pol), out_shap...]
    all_gather x1 -> x0, waiting for transfers between devices: 23.3 us -> none  [on_device(): lax.all_gather(band_rows, ('tile', 'pol'), axis=0, tiled=True)]
    all_to_all x1 -> x0, blocking collectives: 23.1 us -> none  [on_device(): lax.all_to_all(spectra, 'chan', split_axis=3, concat_axis=0, tiled=True)]
    convert_element_type x2 -> x0, local copies, waits for them, and re-layouts: 21.4 us -> none  [the longest x1 16.1 us: make_spectra(): return spectrum.astype(jnp.bfloat16)]
    all_to_all x1 -> x0, local copies, waits for them, and re-layouts: 19.7 us -> none  [on_device(): lax.all_to_all(spectra, 'chan', split_axis=3, concat_axis=0, tiled=True)]
    unnamed x16 -> x19, local copies, waits for them, and re-layouts: 24.6 us -> 9.69 us
    slice x1 -> x0, local copies, waits for them, and re-layouts: 10 us -> none  [make_spectra(): frames_all[:, tap_index:tap_index + FRAMES]]
    dot_general x3 -> x0, matrix products: 7.41 us -> none  [the longest x1 3.36 us: correlate(): jnp.einsum('rik,jk->rij', left_rows, panel_cols, preferred_element_type=j...]
  transfers between devices with their start and end apart: 1 -> 0, of which waited for: 1 -> 0; matrix products, arithmetic and copies ran while one was open for 1% -> 0% of each run, Pallas kernels for 0% -> 0%
where the time goes in v1:
time: 45.1 us; the launch traced here: 44.7 us
  Pallas kernels  35 us (78%)
  local copies, waits for them, and re-layouts  9.69 us (21%)
    pallas_call x1, Pallas kernels, on_device_kernel(): pl.pallas_call(functools.partial(kernel, n_chan, n_tile, n_pol), out_shap...  35 us
    unnamed x19, local copies, waits for them, and re-layouts  9.69 us

profile of v1, /device:TPU:0, one launch (start us, length us, event | category | flops | bytes accessed | tf_op | source)
XLA Modules:
  0.0 44.7 jit_solution(2586637201127892431)
XLA Ops:
  0.0 0.0 copy-start
  0.0 1.4 %copy-done = bf16[1,8,100000]{2,1,0:T(8,128)(2,1)S(1)} copy-done((bf16[1,8,100000]{2,1,0:T(8,128)(2,1)S(1)}, bf16[1,8,100000]{2,1,0:T(8,128)(2,1)}, u32[]{:S(2)}) %copy-start) | copy-done | bytes 1600024
  1.4 0.0 copy-start.1
  1.4 1.1 %copy-done.1 = bf16[640,640]{1,0:T(8,128)(2,1)S(1)} copy-done((bf16[640,640]{1,0:T(8,128)(2,1)S(1)}, bf16[640,640]{1,0:T(8,128)(2,1)}, u32[]{:S(2)}) %copy-start.1) | copy-done | bytes 819224
  2.6 0.0 copy-start.2
  2.6 1.1 %copy-done.2 = bf16[640,640]{1,0:T(8,128)(2,1)S(1)} copy-done((bf16[640,640]{1,0:T(8,128)(2,1)S(1)}, bf16[640,640]{1,0:T(8,128)(2,1)}, u32[]{:S(2)}) %copy-start.2) | copy-done | bytes 819224
  3.7 0.0 copy-start.3
  3.7 1.1 %copy-done.3 = f32[2,2,320,128]{3,2,1,0:T(8,128)S(1)} copy-done((f32[2,2,320,128]{3,2,1,0:T(8,128)S(1)}, f32[2,2,320,128]{3,2,1,0:T(8,128)}, u32[]{:S(2)}) %copy-start.3) | copy-done | bytes 655384
  4.8 0.0 copy-start.4
  4.8 1.1 %copy-done.4 = f32[2,640,128]{2,1,0:T(8,128)S(1)} copy-done((f32[2,640,128]{2,1,0:T(8,128)S(1)}, f32[2,640,128]{2,1,0:T(8,128)}, u32[]{:S(2)}) %copy-start.4) | copy-done | bytes 655384
  5.9 0.0 copy-start.5
  5.9 1.0 %copy-done.5 = bf16[512,512]{1,0:T(8,128)(2,1)S(1)} copy-done((bf16[512,512]{1,0:T(8,128)(2,1)S(1)}, bf16[512,512]{1,0:T(8,128)(2,1)}, u32[]{:S(2)}) %copy-start.5) | copy-done | bytes 524312
  6.9 0.0 copy-start.6
  6.9 0.8 %copy-done.6 = bf16[4,2,16,256]{3,2,1,0:T(8,128)(2,1)S(1)} copy-done((bf16[4,2,16,256]{3,2,1,0:T(8,128)(2,1)S(1)}, bf16[4,2,16,256]{3,2,1,0:T(8,128)(2,1)}, u32[]{:S(2)}) %copy-start.6) | copy-done | bytes 65560
  7.8 0.0 copy-start.7
  7.8 0.7 %copy-done.7 = s32[1,8]{1,0:T(1,128)S(1)} copy-done((s32[1,8]{1,0:T(1,128)S(1)}, s32[1,8]{1,0:T(1,128)}, u32[]{:S(2)}) %copy-start.7) | copy-done | bytes 56
  8.4 0.0 copy-start.8
  8.4 0.7 %copy-done.8 = s32[4]{0:T(128)S(1)} copy-done((s32[4]{0:T(128)S(1)}, s32[4]{0:T(128)}, u32[]{:S(2)}) %copy-start.8) | copy-done | bytes 40
  9.1 35.0 %shard_map.91 = f32[2,1,32,128]{3,2,1,0:T(8,128)S(1)} custom-call(bf16[1,8,100000]{2,1,0:T(8,128)(2,1)S(1)} %copy-done, s32[1,8]{1,0:T(1,128)S(1)} %copy-done.7, s32[4]{0:T(128)S(1)} %copy-done.8, f32[2,640,128]{2,1,0:T(8,128)S(1)} %copy-done.4, bf16[640,640]{1,0:T(8,128)(2,1)S(1)} %copy-done.2, bf16[640,640]{1,0:T(8,128)(2,1)S(1)} %copy-done.1, ...), custom_call_target="tpu_custom_call" | custom-call | tf_op jit(solution)/shard_map/pallas_call | solution.py:356
  44.1 0.6 %copy.11 = f32[2,1,32,128]{3,2,1,0:T(8,128)} copy(f32[2,1,32,128]{3,2,1,0:T(8,128)S(1)} %shard_map.91) | data formatting | bytes 65536
Async XLA Ops:
  0.0 1.4 %copy-start = (bf16[1,8,100000]{2,1,0:T(8,128)(2,1)S(1)}, bf16[1,8,100000]{2,1,0:T(8,128)(2,1)}, u32[]{:S(2)}) copy-start(bf16[1,8,100000]{2,1,0:T(8,128)(2,1)} %volt_ref.1) | copy-start | bytes 4800004
  1.4 1.1 %copy-start.1 = (bf16[640,640]{1,0:T(8,128)(2,1)S(1)}, bf16[640,640]{1,0:T(8,128)(2,1)}, u32[]{:S(2)}) copy-start(bf16[640,640]{1,0:T(8,128)(2,1)} %constant.14.clone.dl_ref) | copy-start | bytes 2457604
  2.6 1.1 %copy-start.2 = (bf16[640,640]{1,0:T(8,128)(2,1)S(1)}, bf16[640,640]{1,0:T(8,128)(2,1)}, u32[]{:S(2)}) copy-start(bf16[640,640]{1,0:T(8,128)(2,1)} %constant.13.clone.dh_ref) | copy-start | bytes 2457604
  3.7 1.1 %copy-start.3 = (f32[2,2,320,128]{3,2,1,0:T(8,128)S(1)}, f32[2,2,320,128]{3,2,1,0:T(8,128)}, u32[]{:S(2)}) copy-start(f32[2,2,320,128]{3,2,1,0:T(8,128)} %constant.15.clone.twist_ref) | copy-start | bytes 1966084
  4.8 1.1 %copy-start.4 = (f32[2,640,128]{2,1,0:T(8,128)S(1)}, f32[2,640,128]{2,1,0:T(8,128)}, u32[]{:S(2)}) copy-start(f32[2,640,128]{2,1,0:T(8,128)} %constant.12.clone.win_ref) | copy-start | bytes 1966084
  5.9 1.0 %copy-start.5 = (bf16[512,512]{1,0:T(8,128)(2,1)S(1)}, bf16[512,512]{1,0:T(8,128)(2,1)}, u32[]{:S(2)}) copy-start(bf16[512,512]{1,0:T(8,128)(2,1)} %constant.17.clone.perm_ref) | copy-start | bytes 1572868
  6.9 0.8 %copy-start.6 = (bf16[4,2,16,256]{3,2,1,0:T(8,128)(2,1)S(1)}, bf16[4,2,16,256]{3,2,1,0:T(8,128)(2,1)}, u32[]{:S(2)}) copy-start(bf16[4,2,16,256]{3,2,1,0:T(8,128)(2,1)} %constant.16.clone.outer_ref) | copy-start | bytes 196612
  7.8 0.7 %copy-start.7 = (s32[1,8]{1,0:T(1,128)S(1)}, s32[1,8]{1,0:T(1,128)}, u32[]{:S(2)}) copy-start(s32[1,8]{1,0:T(1,128)} %flag_ref.1) | copy-start | bytes 100
  8.4 0.7 %copy-start.8 = (s32[4]{0:T(128)S(1)}, s32[4]{0:T(128)}, u32[]{:S(2)}) copy-start(s32[4]{0:T(128)} %table_ref.1) | copy-start | bytes 52

commit v2 on v1

--- a/solution.py
+++ b/solution.py
@@ -177,10 +177,23 @@
 
 
 def kernel(
-    n_chan, n_tile, n_pol, volt_ref, flag_ref, table_ref, win_ref, dh_ref, dl_ref, twist_ref,
-    outer_ref, perm_ref, out_ref, flat, u_high, u_low, zt, turned, send, recv, left, vpart, vrecv,
-    send_sem, recv_sem, vsend_sem, vrecv_sem,
+    n_chan, n_tile, n_pol, volt_hbm, flag_hbm, table_hbm, win_hbm, dh_hbm, dl_hbm, twist_hbm,
+    outer_hbm, perm_hbm, out_ref, volt_ref, flag_ref, table_ref, win_ref, dh_ref, dl_ref, twist_ref,
+    outer_ref, perm_ref, flat, u_high, u_low, zt, turned, send, recv, left, vpart, vrecv,
+    load_sem, send_sem, recv_sem, vsend_sem, vrecv_sem,
 ):
+    loads = [
+        pltpu.make_async_copy(source, target, load_sem.at[n])
+        for n, (source, target) in enumerate(
+            [
+                (volt_hbm, volt_ref), (win_hbm, win_ref), (dh_hbm, dh_ref), (dl_hbm, dl_ref),
+                (twist_hbm, twist_ref), (outer_hbm, outer_ref), (flag_hbm, flag_ref),
+                (table_hbm, table_ref), (perm_hbm, perm_ref),
+            ]
+        )
+    ]
+    for load in loads:
+        load.start()
     n_groups = n_tile * n_pol
     c, t, p = lax.axis_index("chan"), lax.axis_index("tile"), lax.axis_index("pol")
     g = t * n_pol + p
@@ -208,12 +221,12 @@
     flat[pl.ds(tiles_full * IN_DEV, flat.shape[0] - tiles_full * IN_DEV), :] = jnp.zeros(
         (flat.shape[0] - tiles_full * IN_DEV, LANES), jnp.float32
     )
+    step = 71
+    loads[0].wait()
     if rest:
         flat[pl.ds(tiles_full * IN_DEV, IN_DEV), pl.ds(0, rest)] = volt_ref[
             0, :, pl.ds(tiles_full * LANES, rest)
         ].astype(jnp.float32)
-
-    step = 11
 
     def spread(chunk, carry):
         for j in range(step):
@@ -225,6 +238,8 @@
 
     lax.fori_loop(0, tiles_full // step, spread, 0)
 
+    for load in loads[1:8]:
+        load.wait()
     outer_rows = jnp.concatenate(
         [outer_ref[table_ref[b], part] for part in range(2) for b in range(n_chan)], axis=0
     )
@@ -300,6 +315,7 @@
             ).wait()
 
     n_in = n_groups * n_chan * IN_DEV
+    loads[8].wait()
     got = recv[...].reshape(4 * n_in, WIDE)
     for q in range(4):
         part = jnp.dot(
@@ -349,16 +365,18 @@
     n_in = n_src * IN_DEV
     consts = [jnp.asarray(x) for x in tables(n_groups, n_chan)]
     vmem = pl.BlockSpec(memory_space=pltpu.VMEM)
-    smem = pl.BlockSpec(memory_space=pltpu.SMEM)
+    operands = [voltages, flagged, channel_table, *consts]
+    spaces = [pltpu.VMEM, pltpu.SMEM, pltpu.SMEM] + [pltpu.VMEM] * len(consts)
     rows = n_in // n_groups
     tiles = -(-voltages.shape[2] // LANES)
     tall = max(tiles, N_OUTER * N_INNER // LANES + A_PAD)
     return pl.pallas_call(
         functools.partial(kernel, n_chan, n_tile, n_pol),
         out_shape=jax.ShapeDtypeStruct((2, 1, rows, n_in), jnp.float32),
-        in_specs=[vmem, smem, smem] + [vmem] * 6,
+        in_specs=[pl.BlockSpec(memory_space=pl.ANY)] * len(operands),
         out_specs=vmem,
-        scratch_shapes=[
+        scratch_shapes=[space(x.shape, x.dtype) for space, x in zip(spaces, operands)]
+        + [
             pltpu.VMEM((tall * IN_DEV, LANES), jnp.float32),
             pltpu.VMEM((A_PAD, HALF_IN * FRAMES * LANES), jnp.bfloat16),
             pltpu.VMEM((A_PAD, HALF_IN * FRAMES * LANES), jnp.bfloat16),
@@ -369,15 +387,16 @@
             pltpu.VMEM((2 * n_in, 4 * WIDE), jnp.bfloat16),
             pltpu.VMEM((n_groups, 2 * rows, n_in), jnp.float32),
             pltpu.VMEM((n_groups - 1, 2 * rows, n_in), jnp.float32),
+            pltpu.SemaphoreType.DMA((len(operands),)),
             pltpu.SemaphoreType.DMA((2, n_src - 1)),
             pltpu.SemaphoreType.DMA((2, n_src - 1)),
             pltpu.SemaphoreType.DMA((n_groups - 1,)),
             pltpu.SemaphoreType.DMA((n_groups - 1,)),
         ],
         compiler_params=pltpu.CompilerParams(
-            collective_id=0, has_side_effects=True, vmem_limit_bytes=48 * 1024 * 1024
+            collective_id=0, has_side_effects=True, vmem_limit_bytes=60 * 1024 * 1024
         ),
-    )(voltages, flagged, channel_table, *consts)
+    )(*operands)
 
 
 def solution(mesh):

time: 45.1 us -> 37.4 us (0.83)
  local copies, waits for them, and re-layouts: 9.69 us -> 1.38 us
  Pallas kernels: 35 us -> 35.8 us
    unnamed x19 -> x1, local copies, waits for them, and re-layouts: 9.69 us -> 1.38 us
    pallas_call x1, Pallas kernels: 35 us -> 35.8 us  [on_device_kernel(): pl.pallas_call(functools.partial(kernel, n_chan, n_tile, n_pol), out_shap...]
where the time goes in v2:
time: 37.4 us; the launch traced here: 37.2 us
  Pallas kernels  35.8 us (96%)
  local copies, waits for them, and re-layouts  1.38 us (4%)
    pallas_call x1, Pallas kernels, on_device_kernel(): pl.pallas_call(functools.partial(kernel, n_chan, n_tile, n_pol), out_shap...  35.8 us
    unnamed x1, local copies, waits for them, and re-layouts  1.38 us

profile of v2, /device:TPU:0, one launch (start us, length us, event | category | flops | bytes accessed | tf_op | source)
XLA Modules:
  0.0 37.2 jit_solution(12273803399411774248)
XLA Ops:
  0.0 35.8 %shard_map.91 = f32[2,1,32,128]{3,2,1,0:T(8,128)} custom-call(bf16[1,8,100000]{2,1,0:T(8,128)(2,1)} %volt_hbm.1, s32[1,8]{1,0:T(1,128)} %flag_hbm.1, s32[4]{0:T(128)} %table_hbm.1, f32[2,640,128]{2,1,0:T(8,128)} %constant.12.clone.win_hbm, bf16[640,640]{1,0:T(8,128)(2,1)} %constant.13.clone.dh_hbm, bf16[640,640]{1,0:T(8,128)(2,1)} %constant.14.clone.dl_hbm, ...), custom_call_target="tpu_custom_call" | custom-call | tf_op jit(solution)/shard_map/pallas_call | solution.py:373
  35.8 1.4 %copy.11 = f32[2,1,32,128]{3,2,1,0:T(8,128)} copy(f32[2,1,32,128]{3,2,1,0:T(8,128)} %shard_map.91) | data formatting | bytes 65536

commit v3 on v2

--- a/solution.py
+++ b/solution.py
@@ -172,21 +172,20 @@
                     perm[q, src * IN_DEV + h * HALF_IN + i, h, src, q, i] = 1.0
     size = 4 * n_src * IN_DEV
     perm = perm.reshape(size, size).astype(jnp.bfloat16)
-    dft_high, dft_low = split_bf16(dft)
-    return win.astype(np.float32), dft_high, dft_low, twist.astype(np.float32), outer, perm
+    return win.astype(np.float32), dft.astype(jnp.bfloat16), twist.astype(np.float32), outer, perm
 
 
 def kernel(
-    n_chan, n_tile, n_pol, volt_hbm, flag_hbm, table_hbm, win_hbm, dh_hbm, dl_hbm, twist_hbm,
-    outer_hbm, perm_hbm, out_ref, volt_ref, flag_ref, table_ref, win_ref, dh_ref, dl_ref, twist_ref,
-    outer_ref, perm_ref, flat, u_high, u_low, zt, turned, send, recv, left, vpart, vrecv,
+    n_chan, n_tile, n_pol, volt_hbm, flag_hbm, table_hbm, win_hbm, dh_hbm, twist_hbm,
+    outer_hbm, perm_hbm, out_ref, volt_ref, flag_ref, table_ref, win_ref, dh_ref, twist_ref,
+    outer_ref, perm_ref, flat, u_all, zt, turned, send, recv, left, vpart, vrecv,
     load_sem, send_sem, recv_sem, vsend_sem, vrecv_sem,
 ):
     loads = [
         pltpu.make_async_copy(source, target, load_sem.at[n])
         for n, (source, target) in enumerate(
             [
-                (volt_hbm, volt_ref), (win_hbm, win_ref), (dh_hbm, dh_ref), (dl_hbm, dl_ref),
+                (volt_hbm, volt_ref), (win_hbm, win_ref), (dh_hbm, dh_ref),
                 (twist_hbm, twist_ref), (outer_hbm, outer_ref), (flag_hbm, flag_ref),
                 (table_hbm, table_ref), (perm_hbm, perm_ref),
             ]
@@ -201,7 +200,7 @@
 
     def peers():
         found = []
-        for dc in range(n_chan - 1, -1, -1):
+        for dc in sorted(range(n_chan), key=lambda dc: (dc == 0, abs(2 * dc - n_chan))):
             for dt in range(n_tile - 1, -1, -1):
                 for dp in range(n_pol - 1, -1, -1):
                     if dc or dt or dp:
@@ -238,7 +237,7 @@
 
     lax.fori_loop(0, tiles_full // step, spread, 0)
 
-    for load in loads[1:8]:
+    for load in loads[1:7]:
         load.wait()
     outer_rows = jnp.concatenate(
         [outer_ref[table_ref[b], part] for part in range(2) for b in range(n_chan)], axis=0
@@ -256,20 +255,13 @@
                 first = s * shift * IN_DEV + h * HALF_IN + i
                 col = (i * FRAMES + s) * LANES
                 u = flat[pl.ds(first, A_PAD, stride=IN_DEV), :] * win_ref[s]
-                high = u.astype(jnp.bfloat16)
-                u_high[:, col : col + LANES] = high
-                u_low[:, col : col + LANES] = (u - high.astype(jnp.float32)).astype(jnp.bfloat16)
+                u_all[h, :, col : col + LANES] = u.astype(jnp.bfloat16)
         for i in range(HALF_IN):
             for s in range(FRAMES):
                 col = (i * FRAMES + s) * LANES
                 if s == 0:
                     wide = pl.ds(i * FRAMES * LANES, FRAMES * LANES)
-                    uh, ul = u_high[:, wide], u_low[:, wide]
-                    y = (
-                        jnp.dot(dh_ref[...], uh, preferred_element_type=jnp.float32)
-                        + jnp.dot(dl_ref[...], uh, preferred_element_type=jnp.float32)
-                        + jnp.dot(dh_ref[...], ul, preferred_element_type=jnp.float32)
-                    )
+                    y = jnp.dot(dh_ref[...], u_all[h, :, wide], preferred_element_type=jnp.float32)
                 yr = y[:K0_PAD, s * LANES : (s + 1) * LANES]
                 yi = y[K0_PAD:, s * LANES : (s + 1) * LANES]
                 co, si = twist_ref[s, 0], twist_ref[s, 1]
@@ -302,6 +294,9 @@
             ).start()
         recv[h, src] = send[h, c * n_groups + g]
 
+    loads[7].wait()
+    n_in = n_groups * n_chan * IN_DEV
+    half_rows = n_groups * n_chan * ROWS
     for h in range(2):
         for d, peer in enumerate(everyone):
             slot = peer[0] * n_groups + peer[1] * n_pol + peer[2]
@@ -313,19 +308,19 @@
                 device_id=where(peer),
                 device_id_type=MESH,
             ).wait()
-
-    n_in = n_groups * n_chan * IN_DEV
-    loads[8].wait()
-    got = recv[...].reshape(4 * n_in, WIDE)
-    for q in range(4):
-        part = jnp.dot(
-            perm_ref[pl.ds(q * n_in, n_in), :], got, preferred_element_type=jnp.float32
-        ).astype(jnp.bfloat16)
-        left[0:n_in, pl.ds(q * WIDE, WIDE)] = part
-        if q % 2 == 0:
-            left[n_in : 2 * n_in, pl.ds((q + 1) * WIDE, WIDE)] = -part
-        else:
-            left[n_in : 2 * n_in, pl.ds((q - 1) * WIDE, WIDE)] = part
+        got = recv[h].reshape(half_rows, WIDE)
+        for q in range(4):
+            part = jnp.dot(
+                perm_ref[pl.ds(q * n_in, n_in), h * half_rows : (h + 1) * half_rows],
+                got,
+                preferred_element_type=jnp.float32,
+            ).astype(jnp.bfloat16)
+            if h == 1:
+                part = part + left[0:n_in, pl.ds(q * WIDE, WIDE)]
+            left[0:n_in, pl.ds(q * WIDE, WIDE)] = part
+            if h == 1:
+                other = (q + 1) if q % 2 == 0 else (q - 1)
+                left[n_in : 2 * n_in, pl.ds(other * WIDE, WIDE)] = -part if q % 2 == 0 else part
     vis = lax.dot_general(
         left[...], left[0:n_in, :], (((1,), (1,)), ((), ())), preferred_element_type=jnp.float32
     )
@@ -378,8 +373,7 @@
         scratch_shapes=[space(x.shape, x.dtype) for space, x in zip(spaces, operands)]
         + [
             pltpu.VMEM((tall * IN_DEV, LANES), jnp.float32),
-            pltpu.VMEM((A_PAD, HALF_IN * FRAMES * LANES), jnp.bfloat16),
-            pltpu.VMEM((A_PAD, HALF_IN * FRAMES * LANES), jnp.bfloat16),
+            pltpu.VMEM((2, A_PAD, HALF_IN * FRAMES * LANES), jnp.bfloat16),
             pltpu.VMEM((2, WIDE, 2 * LANES), jnp.bfloat16),
             pltpu.VMEM((WIDE // LANES, R_ALL * ROWS, LANES), jnp.float32),
             pltpu.VMEM((2, R_ALL, ROWS, WIDE), jnp.bfloat16),

time: 37.4 us -> 31.1 us (0.83)
  Pallas kernels: 35.8 us -> 29.6 us
    pallas_call x1, Pallas kernels: 35.8 us -> 29.6 us  [on_device_kernel(): pl.pallas_call(functools.partial(kernel, n_chan, n_tile, n_pol), out_shap...]
where the time goes in v3:
time: 31.1 us; the launch traced here: 30.9 us
  Pallas kernels  29.6 us (95%)
  local copies, waits for them, and re-layouts  1.38 us (4%)
    pallas_call x1, Pallas kernels, on_device_kernel(): pl.pallas_call(functools.partial(kernel, n_chan, n_tile, n_pol), out_shap...  29.6 us
    unnamed x1, local copies, waits for them, and re-layouts  1.38 us

profile of v3, /device:TPU:0, one launch (start us, length us, event | category | flops | bytes accessed | tf_op | source)
XLA Modules:
  0.0 30.9 jit_solution(12260945487066360581)
XLA Ops:
  0.0 29.6 %shard_map.82 = f32[2,1,32,128]{3,2,1,0:T(8,128)} custom-call(bf16[1,8,100000]{2,1,0:T(8,128)(2,1)} %volt_hbm.1, s32[1,8]{1,0:T(1,128)} %flag_hbm.1, s32[4]{0:T(128)} %table_hbm.1, f32[2,640,128]{2,1,0:T(8,128)} %constant.10.clone.win_hbm, bf16[640,640]{1,0:T(8,128)(2,1)} %constant.11.clone.dh_hbm, f32[2,2,320,128]{3,2,1,0:T(8,128)} %constant.12.clone.twist_hbm, ...), custom_call_target="tpu_custom_call" | custom-call | tf_op jit(solution)/shard_map/pallas_call | solution.py:368
  29.6 1.4 %copy.10 = f32[2,1,32,128]{3,2,1,0:T(8,128)} copy(f32[2,1,32,128]{3,2,1,0:T(8,128)} %shard_map.82) | data formatting | bytes 65536

commit v4 on v3

--- a/solution.py
+++ b/solution.py
@@ -114,6 +114,8 @@
 K0_PAD = 320
 R_ALL = 16
 IN_DEV = 8
+PITCH = 9
+SPLIT = 2
 HALF_IN = 4
 ROWS = 16
 WIDE = FRAMES * K0_PAD
@@ -211,19 +213,40 @@
         return {"chan": peer[0], "tile": peer[1], "pol": peer[2]}
 
     everyone = peers()
+    early = SPLIT * n_groups
+    moves = [[], []]
+    for d, peer in enumerate(everyone):
+        slot = peer[0] * n_groups + peer[1] * n_pol + peer[2]
+        for h in range(2):
+            if d < early:
+                source, target = send.at[slot, h], recv.at[src, h]
+            elif h == 1:
+                source, target = send.at[slot], recv.at[src]
+            else:
+                continue
+            moves[h].append(
+                pltpu.make_async_remote_copy(
+                    src_ref=source,
+                    dst_ref=target,
+                    send_sem=send_sem.at[h, d],
+                    recv_sem=recv_sem.at[h, d],
+                    device_id=where(peer),
+                    device_id_type=MESH,
+                )
+            )
     barrier = pltpu.get_barrier_semaphore()
     for peer in everyone:
         pl.semaphore_signal(barrier, inc=1, device_id=where(peer), device_id_type=MESH)
 
     tiles_full = volt_ref.shape[2] // LANES
     rest = volt_ref.shape[2] - tiles_full * LANES
-    flat[pl.ds(tiles_full * IN_DEV, flat.shape[0] - tiles_full * IN_DEV), :] = jnp.zeros(
-        (flat.shape[0] - tiles_full * IN_DEV, LANES), jnp.float32
+    flat[pl.ds(tiles_full * PITCH, flat.shape[0] - tiles_full * PITCH), :] = jnp.zeros(
+        (flat.shape[0] - tiles_full * PITCH, LANES), jnp.float32
     )
     step = 71
     loads[0].wait()
     if rest:
-        flat[pl.ds(tiles_full * IN_DEV, IN_DEV), pl.ds(0, rest)] = volt_ref[
+        flat[pl.ds(tiles_full * PITCH, IN_DEV), pl.ds(0, rest)] = volt_ref[
             0, :, pl.ds(tiles_full * LANES, rest)
         ].astype(jnp.float32)
 
@@ -231,7 +254,7 @@
         for j in range(step):
             tile = chunk * step + j
             lane = pl.multiple_of(tile * LANES, LANES)
-            row = pl.multiple_of(tile * IN_DEV, IN_DEV)
+            row = tile * PITCH
             flat[pl.ds(row, IN_DEV), :] = volt_ref[0, :, pl.ds(lane, LANES)].astype(jnp.float32)
         return carry
 
@@ -252,9 +275,9 @@
     for h in range(2):
         for i in range(HALF_IN):
             for s in range(FRAMES):
-                first = s * shift * IN_DEV + h * HALF_IN + i
+                first = s * shift * PITCH + h * HALF_IN + i
                 col = (i * FRAMES + s) * LANES
-                u = flat[pl.ds(first, A_PAD, stride=IN_DEV), :] * win_ref[s]
+                u = flat[pl.ds(first, A_PAD, stride=PITCH), :] * win_ref[s]
                 u_all[h, :, col : col + LANES] = u.astype(jnp.bfloat16)
         for i in range(HALF_IN):
             for s in range(FRAMES):
@@ -277,38 +300,22 @@
             for l in range(WIDE // LANES):
                 turned[l, pl.ds(i, n_rows, stride=HALF_IN), :] = x[:, l * LANES : (l + 1) * LANES]
         for l in range(WIDE // LANES):
-            send[h, :, :, pl.ds(l * LANES, LANES)] = (
+            send[:, h, :, pl.ds(l * LANES, LANES)] = (
                 turned[l].astype(jnp.bfloat16).reshape(R_ALL, ROWS, LANES)
             )
         if h == 0:
             pl.semaphore_wait(barrier, len(everyone))
-        for d, peer in enumerate(everyone):
-            slot = peer[0] * n_groups + peer[1] * n_pol + peer[2]
-            pltpu.make_async_remote_copy(
-                src_ref=send.at[h, slot],
-                dst_ref=recv.at[h, src],
-                send_sem=send_sem.at[h, d],
-                recv_sem=recv_sem.at[h, d],
-                device_id=where(peer),
-                device_id_type=MESH,
-            ).start()
-        recv[h, src] = send[h, c * n_groups + g]
+        for move in moves[h]:
+            move.start()
+        recv[src, h] = send[c * n_groups + g, h]
 
     loads[7].wait()
     n_in = n_groups * n_chan * IN_DEV
     half_rows = n_groups * n_chan * ROWS
+    for move in moves[0] + moves[1]:
+        move.wait()
     for h in range(2):
-        for d, peer in enumerate(everyone):
-            slot = peer[0] * n_groups + peer[1] * n_pol + peer[2]
-            pltpu.make_async_remote_copy(
-                src_ref=send.at[h, slot],
-                dst_ref=recv.at[h, src],
-                send_sem=send_sem.at[h, d],
-                recv_sem=recv_sem.at[h, d],
-                device_id=where(peer),
-                device_id_type=MESH,
-            ).wait()
-        got = recv[h].reshape(half_rows, WIDE)
+        got = recv[:, h].reshape(half_rows, WIDE)
         for q in range(4):
             part = jnp.dot(
                 perm_ref[pl.ds(q * n_in, n_in), h * half_rows : (h + 1) * half_rows],
@@ -372,12 +379,12 @@
         out_specs=vmem,
         scratch_shapes=[space(x.shape, x.dtype) for space, x in zip(spaces, operands)]
         + [
-            pltpu.VMEM((tall * IN_DEV, LANES), jnp.float32),
+            pltpu.VMEM((tall * PITCH, LANES), jnp.float32),
             pltpu.VMEM((2, A_PAD, HALF_IN * FRAMES * LANES), jnp.bfloat16),
             pltpu.VMEM((2, WIDE, 2 * LANES), jnp.bfloat16),
             pltpu.VMEM((WIDE // LANES, R_ALL * ROWS, LANES), jnp.float32),
-            pltpu.VMEM((2, R_ALL, ROWS, WIDE), jnp.bfloat16),
-            pltpu.VMEM((2, n_src, ROWS, WIDE), jnp.bfloat16),
+            pltpu.VMEM((R_ALL, 2, ROWS, WIDE), jnp.bfloat16),
+            pltpu.VMEM((n_src, 2, ROWS, WIDE), jnp.bfloat16),
             pltpu.VMEM((2 * n_in, 4 * WIDE), jnp.bfloat16),
             pltpu.VMEM((n_groups, 2 * rows, n_in), jnp.float32),
             pltpu.VMEM((n_groups - 1, 2 * rows, n_in), jnp.float32),

time: 31.1 us -> 29.7 us (0.955)
  Pallas kernels: 29.6 us -> 28.1 us
    pallas_call x1, Pallas kernels: 29.6 us -> 28.1 us  [on_device_kernel(): pl.pallas_call(functools.partial(kernel, n_chan, n_tile, n_pol), out_shap...]
where the time goes in v4:
time: 29.7 us; the launch traced here: 29.5 us
  Pallas kernels  28.1 us (95%)
  local copies, waits for them, and re-layouts  1.38 us (5%)
    pallas_call x1, Pallas kernels, on_device_kernel(): pl.pallas_call(functools.partial(kernel, n_chan, n_tile, n_pol), out_shap...  28.1 us
    unnamed x1, local copies, waits for them, and re-layouts  1.38 us

profile of v4, /device:TPU:0, one launch (start us, length us, event | category | flops | bytes accessed | tf_op | source)
XLA Modules:
  0.0 29.5 jit_solution(18134567877117288605)
XLA Ops:
  0.0 28.1 %shard_map.82 = f32[2,1,32,128]{3,2,1,0:T(8,128)} custom-call(bf16[1,8,100000]{2,1,0:T(8,128)(2,1)} %volt_hbm.1, s32[1,8]{1,0:T(1,128)} %flag_hbm.1, s32[4]{0:T(128)} %table_hbm.1, f32[2,640,128]{2,1,0:T(8,128)} %constant.10.clone.win_hbm, bf16[640,640]{1,0:T(8,128)(2,1)} %constant.11.clone.dh_hbm, f32[2,2,320,128]{3,2,1,0:T(8,128)} %constant.12.clone.twist_hbm, ...), custom_call_target="tpu_custom_call" | custom-call | tf_op jit(solution)/shard_map/pallas_call | solution.py:375
  28.1 1.4 %copy.10 = f32[2,1,32,128]{3,2,1,0:T(8,128)} copy(f32[2,1,32,128]{3,2,1,0:T(8,128)} %shard_map.82) | data formatting | bytes 65536
